TPU v7x, 128 devices: a whole 4x4x4 slice. The times are simulated.
128 devices in a mesh: rows: 64 (over x, y_lo, z, core), chan: 2 (over y_hi).
Axes of the slice: x: 4, y: 4 (y_hi: 2, y_lo: 2; y = y_hi * 2 + y_lo), z: 4, core: 2. Of those that a mesh axis runs over, the one named last changes fastest.
Arguments:
- spectra: bfloat16 [1024, 512, 2048], P('rows', None, 'chan'), may hold values from -40 to 40
- factors: bfloat16 [2048, 128], P('chan'), may hold values from -0.125 to 0.125
Outputs:
- scaled_gradient: float32 [128, 2048], P('rows', 'chan')
- objective: float32 [1], replicated
All inputs are finite; a program needn't handle non-finite values.
Results may differ from a plain program's by a relative error of at most 0.0029.
Values may be sent and summed in bfloat16 or wider, within the bound.
A program may use at most 128 MiB of HBM per device.

v0:
```python
import jax
import jax.numpy as jnp
from jax import lax
from jax.sharding import PartitionSpec as P


def padded_2(cells, sides, width):
    for axis, dim in sides:
        count = lax.axis_size(axis)
        ends = count - 1
        head = lax.slice_in_dim(cells, 0, width, axis=dim)
        tail = lax.slice_in_dim(cells, cells.shape[dim] - width, cells.shape[dim], axis=dim)
        cells = jnp.concatenate(
            [
                lax.ppermute(tail, axis, [(i, (i + 1) % count) for i in range(ends)]),
                cells,
                lax.ppermute(head, axis, [((i + 1) % count, i) for i in range(ends)]),
            ],
            axis=dim,
        )
    return cells


def on_device(spectra, factors):
    rows_here, swath_cols, channel_count = spectra.shape
    pixel_rows = spectra.reshape(rows_here * swath_cols, channel_count)
    partial_scores = jnp.dot(pixel_rows, factors, preferred_element_type=jnp.float32)
    scores = lax.psum(partial_scores, "chan")
    factor_count = scores.shape[1]
    score_grid = scores.reshape(rows_here, swath_cols, factor_count)
    padded = padded_2(score_grid, (("rows", 0),), 4)
    total_rows = rows_here * lax.axis_size("rows")
    first_row = lax.axis_index("rows") * rows_here
    global_rows = first_row + jnp.arange(rows_here, dtype=jnp.int32)
    npix = float(total_rows * swath_cols)
    lag_terms = []
    pair_counts = []
    lag_grad = jnp.zeros_like(score_grid)
    for distance in range(1, 5):
        ahead_rows = padded[4 + distance : 4 + distance + rows_here]
        behind_rows = padded[4 - distance : 4 - distance + rows_here]
        fwd_ok = (global_rows + distance < total_rows).astype(jnp.float32)[:, None, None]
        back_ok = (global_rows >= distance).astype(jnp.float32)[:, None, None]
        forward_diff = (ahead_rows - score_grid) * fwd_ok
        pair_count = float((total_rows - distance) * swath_cols)
        pair_counts.append(pair_count)
        lag_terms.append(jnp.sum(forward_diff * forward_diff, axis=(0, 1)))
        lag_grad = lag_grad + ((score_grid - behind_rows) * back_ok - forward_diff) / pair_count
    column_sum = jnp.sum(score_grid, axis=(0, 1))
    column_total = lax.psum(column_sum, "rows")
    column_mean = column_total / npix
    centered = score_grid - column_mean
    centered_sq = jnp.sum(centered * centered, axis=(0, 1))
    moments = lax.psum(jnp.stack([centered_sq] + lag_terms), "rows")
    spread = moments[0]
    variogram = jnp.float32(0.0)
    for distance in range(1, 5):
        variogram = variogram + jnp.sum(moments[distance]) / (2.0 * pair_counts[distance - 1])
    cov_total = jnp.sum(spread) / npix
    objective = variogram / cov_total
    weights = (
        npix * lag_grad / cov_total - 2.0 * variogram * centered / (cov_total * cov_total)
    ).astype(jnp.bfloat16)
    weight_rows = weights.reshape(rows_here * swath_cols, factor_count)
    gradient_share = lax.psum_scatter(
        lax.dot_general(
            weight_rows, pixel_rows, (((0,), (0,)), ((), ())), preferred_element_type=jnp.float32
        ),
        "rows",
        scatter_dimension=0,
        tiled=True,
    )
    return (gradient_share, objective.reshape(1))


def solution(mesh):
    in_specs = (P("rows", None, "chan"), P("chan", None))
    out_specs = (P("rows", "chan"), P())
    return jax.shard_map(
        on_device, mesh=mesh, in_specs=in_specs, out_specs=out_specs, check_vma=False
    )
```

profile of v0, /device:TPU:1, one launch (start us, length us, event | category | flops | bytes accessed | tf_op | source)
XLA Modules:
  0.0 1019.8 jit_solution(12881483365225361218)
XLA Ops:
  7.2 0.0 copy-start
  7.2 0.0 all-reduce.4.cloned.1.call-start
  7.2 0.9 copy-done
  8.1 10.1 fusion.55
  18.3 0.0 all-reduce.4.cloned.1.call-update
  18.3 0.0 all-reduce.6.cloned.1.call-start
  18.3 119.3 %all-reduce.4.cloned.1.call-done = f32[8192,128]{1,0:T(8,128)} async-done(((f32[8192,128]{1,0:T(8,128)}), f32[8192,128]{1,0:T(8,128)}) %all-reduce.4.cloned.1.call-update) | async-done | bytes 4194320 | tf_op jit(solution)/shard_map/psum | solution.py:28
  137.6 1.7 fusion.54
  139.3 0.3 copy.20
  139.6 2.6 collective-permute-start.1
  142.3 0.3 copy.17
  142.6 3.1 collective-permute-start
  145.7 5.4 copy.19
  151.1 3.3 reduce_sum.99
  154.3 137.4 %psum.22 = f32[128]{0:T(128)S(1)} all-reduce(f32[128]{0:T(128)S(1)} %reduce_sum.99), channel_id=1, replica_groups=mesh['rows'=64,'chan'=2] {'rows'}, use_global_device_ids=true, to_apply=%region_2.0 | all-reduce | flops 128 | bytes 1024 | tf_op jit(solution)/shard_map/psum | solution.py:50
  291.8 3.4 multiply_reduce_fusion.1
  295.2 4.5 multiply_reduce_fusion
  299.7 143.3 %psum.23 = f32[5,128]{1,0:T(8,128)S(1)} all-reduce(f32[5,128]{1,0:T(8,128)S(1)} %stack.23), channel_id=1, replica_groups=mesh['rows'=64,'chan'=2] {'rows'}, use_global_device_ids=true, to_apply=%region_8.0 | all-reduce | flops 640 | bytes 5120 | tf_op jit(solution)/shard_map/psum | solution.py:54
  443.0 0.7 slice_reduce_fusion
  448.3 24.3 %fusion.45 = f32[128,1024]{1,0:T(8,128)} fusion(bf16[16,512,1024]{2,1,0:T(8,128)(2,1)} %param.2, f32[16,512,128]{1,2,0:T(8,128)} %copy.19, f32[4,512,128]{1,2,0:T(8,128)S(1)} %collective-permute-done, f32[4,512,128]{1,2,0:T(8,128)} %collective-permute-done.1, f32[]{:T(128)S(6)} %mul.127, f32[128]{0:T(128)S(1)} %broadcast_multiply_fusion, ...), kind=kOutput, calls=%fused_computation.60 | convolution fusion | flops 2191523840 | bytes 23593996 | tf_op jit(solution)/shard_map/dot_general | solution.py:66
  472.6 0.0 all-reduce.6.cloned.1.call-update
  472.7 0.6 dynamic-slice
  473.9 536.6 %all-reduce.6.cloned.1.call-done = f32[128,1024]{1,0:T(8,128)} async-done(((f32[128,1024]{1,0:T(8,128)}), f32[128,1024]{1,0:T(8,128)}) %all-reduce.6.cloned.1.call-update) | async-done | bytes 524304
  1010.5 1.4 constant_dynamic-slice_fusion
  (12 shorter events, 0.1 us)
Async XLA Ops:
  7.2 1.0 copy-start
  7.2 130.4 %all-reduce.4.cloned.1.call-start = ((), (), s32[]{:S(2)}) async-start(), calls=%async_computation | async-start | bytes 8388608 | tf_op jit(solution)/shard_map/psum | solution.py:28
  18.3 992.2 %all-reduce.6.cloned.1.call-start = ((), (), s32[]{:S(2)}) async-start(), calls=%async_computation.1 | async-start | bytes 1048576
  139.6 155.6 %collective-permute-start.1 = (f32[4,512,128]{1,2,0:T(8,128)S(1)}, f32[4,512,128]{1,2,0:T(8,128)}, u32[]{:S(2)}, u32[]{:S(2)}) collective-permute-start(f32[4,512,128]{1,2,0:T(8,128)S(1)} %copy.20), channel_id=1, source_target_pairs={{2,0},{4,2},{6,4},{8,6},{10,8},{12,10},{14,12},{16,14},{18,16},{20... | collective-permute-start | bytes 3145736 | tf_op jit(solution)/shard_map/ppermute | solution.py:17
  142.6 305.7 %collective-permute-start = (f32[4,512,128]{1,2,0:T(8,128)S(1)}, f32[4,512,128]{1,2,0:T(8,128)S(1)}, u32[]{:S(2)}, u32[]{:S(2)}) collective-permute-start(f32[4,512,128]{1,2,0:T(8,128)S(1)} %copy.17), channel_id=1, source_target_pairs={{0,2},{2,4},{4,6},{6,8},{8,10},{10,12},{12,14},{14,16},{16,18},{18... | collective-permute-start | bytes 3145736 | tf_op jit(solution)/shard_map/ppermute | solution.py:15
  291.8 3.4 copy-start.1
  448.3 24.4 %copy-start.2 = (u32[128]{0:T(128)S(1)}, u32[128]{0:T(128)}, u32[]{:S(2)}) copy-start(u32[128]{0:T(128)} %constant.58) | copy-start | bytes 1540
Sparse Core Ops, SparseCore 0:
  18.4 119.1 all-reduce.3
  472.8 537.6 all-reduce.5
where the time goes:
time: 1020 us
  waiting for transfers between devices  656 us (64%)
  blocking collectives  281 us (28%)
  matrix products  34.5 us (3%)
  between operations  20.6 us (2%)
  other arithmetic  11.9 us (1%)
  local copies, waits for them, and re-layouts  10.6 us (1%)
    unnamed x3, waiting for transfers between devices  537 us
    psum x1, blocking collectives, on_device(): moments = lax.psum(jnp.stack([centered_sq] + lag_terms), 'rows')  143 us
    psum x1, blocking collectives, on_device(): column_total = lax.psum(column_sum, 'rows')  137 us
    psum x1, waiting for transfers between devices, on_device(): scores = lax.psum(partial_scores, 'chan')  119 us
    dot_general x1, matrix products, on_device(): lax.dot_general(weight_rows, pixel_rows, (((0,), (0,)), ((), ())), prefer...  24.3 us
  transfers between devices with their start and end apart: 4, of which 2 were waited for; matrix products, arithmetic and copies ran while one was open for 2% of the time, Pallas kernels for 0%

commit v1 on v0

v1 whole, which is shorter than its diff:
```python
import jax
import jax.numpy as jnp
from jax import lax
from jax.experimental import pallas as pl
from jax.experimental.pallas import tpu as pltpu
from jax.sharding import PartitionSpec as P

MESH = pl.DeviceIdType.MESH
F32, BF16 = jnp.float32, jnp.bfloat16

ROWS = 16
STRIPS = 64
WP = 512
HALF = 256
K = 128
CH = 1024
H = ROWS * STRIPS
NPIX = float(H * WP)
LAGS = (1, 2, 3, 4)
PAIRS = tuple(float((H - lag) * WP) for lag in LAGS)
SUB = 64


def device_of(x, y, z, core):
    return ((x * 2 + y % 2) * 4 + z) * 2 + core, y // 2


def fold(block):
    return jnp.sum(block.reshape(block.shape[0] // 8, 8, K), axis=0)


def kernel(
    x_hbm, f_hbm, g_out, obj_out,
    xv, fv, fp, s, psend, precv, hsend, hrecv, w, wrecv, mu, acc, tile, mom_a, mom_b, grad,
    red_z, red_x, part, red_b,
    x_sem, f_sem, p_ssem, p_rsem, h_ssem, h_rsem, ma_ssem, ma_rsem, mb_ssem, mb_rsem,
    w_ssem, w_rsem, z_ssem, z_rsem, xx_ssem, xx_rsem, b_ssem, b_rsem,
):
    strip = lax.axis_index("rows")
    chan = lax.axis_index("chan")
    core, z, ylo, xx = strip % 2, (strip // 2) % 4, (strip // 8) % 2, strip // 16
    y = chan * 2 + ylo
    mine = pl.multiple_of(chan * HALF, HALF)
    theirs = pl.multiple_of((1 - chan) * HALF, HALF)
    partner = (strip, 1 - chan)
    after = ((strip + 1) % STRIPS, chan)
    before = ((strip + STRIPS - 1) % STRIPS, chan)

    def order(i):
        return (i + 12) % ROWS

    def x_copy(i, own):
        r, at = order(i), mine if own else theirs
        return pltpu.make_async_copy(
            x_hbm.at[r, pl.ds(at, HALF), :],
            xv.at[r, pl.ds(at, HALF), :],
            x_sem.at[i + (ROWS if own else 0)],
        )

    f_copy = pltpu.make_async_copy(f_hbm, fv, f_sem)
    f_copy.start()

    @pl.loop(0, ROWS)
    def _(i):
        x_copy(i, False).start()
        x_copy(i, True).start()

    barrier = pltpu.get_barrier_semaphore()

    def greet(place):
        pl.semaphore_signal(barrier, inc=1, device_id=place, device_id_type=MESH)

    q = z * 2 + core
    t = xx * 4 + y
    u = xx * 2 + core

    def zc_peer(j):
        other = (q + j) % 8
        return device_of(xx, y, other // 2, other % 2)

    def xy_peer(j):
        other = (t + j) % 16
        return device_of(other // 4, other % 4, z, core)

    def xc_peer(j):
        other = (u + j) % 8
        return device_of(other // 2, y, z, other % 2)

    @pl.loop(1, 8)
    def _(j):
        greet(zc_peer(j))

    @pl.loop(1, 16)
    def _(j):
        greet(xy_peer(j))

    @pl.loop(1, 4)
    def _(j):
        greet(device_of((xx + j) % 4, y, z, 1 - core))
        greet(device_of(xx, chan * 2 + 1 - ylo, (z + j) % 4, core))

    greet(after)
    greet(before)

    f_copy.wait()
    src = lax.broadcasted_iota(jnp.int32, (K, K), 0)
    dst = lax.broadcasted_iota(jnp.int32, (K, K), 1)
    hi, mid, lo, e = dst >> 6, (dst >> 3) & 7, (dst >> 1) & 3, dst & 1
    to_x = jnp.where(hi == 0, lo, mid >> 1)
    to_z = jnp.where(hi == 0, mid >> 1, lo)
    from_k = (((to_x * 2 + hi) * 4 + to_z) * 2 + (mid & 1)) * 2 + e
    permutation = jnp.where(src == from_k, 1.0, 0.0).astype(BF16)
    fp[...] = jnp.dot(fv[...], permutation, preferred_element_type=F32).astype(BF16)

    def p_copy(r):
        return pltpu.make_async_remote_copy(
            psend.at[r], precv.at[r], p_ssem.at[r], p_rsem.at[r],
            device_id=partner, device_id_type=MESH,
        )

    @pl.loop(0, ROWS)
    def _(i):
        r = order(i)
        x_copy(i, False).wait()
        psend[r] = jnp.dot(
            xv[r, pl.ds(theirs, HALF), :], fp[...], preferred_element_type=F32
        ).astype(BF16)

        @pl.when(i == 0)
        def _():
            pl.semaphore_wait(barrier, 30)

        p_copy(r).start()
        x_copy(i, True).wait()
        s[4 + r] = jnp.dot(xv[r, pl.ds(mine, HALF), :], fp[...], preferred_element_type=F32)

    acc[...] = jnp.zeros_like(acc)

    def add_row(r, first=False):
        p_copy(r).wait_recv()
        if first:
            total = jnp.zeros((8, K), F32)
            for h in range(0, HALF, SUB):
                total += fold(s[4 + r, h : h + SUB, :] + precv[r, h : h + SUB, :].astype(F32))
            mu[...] = jnp.broadcast_to(
                jnp.sum(total, axis=0, keepdims=True) * (1.0 / HALF), (8, K)
            )
        shift = mu[0:1, :]
        one, two = jnp.zeros((8, K), F32), jnp.zeros((8, K), F32)
        for h in range(0, HALF, SUB):
            v = s[4 + r, h : h + SUB, :] + precv[r, h : h + SUB, :].astype(F32)
            s[4 + r, h : h + SUB, :] = v
            d = v - shift
            one += fold(d)
            two += fold(d * d)
        acc[0] += one
        acc[1] += two

    def add_lags(a, across=None):
        sums = [jnp.zeros((8, K), F32) for _ in LAGS]
        for h in range(0, HALF, SUB):
            here = s[4 + a, h : h + SUB, :]
            for n, lag in enumerate(LAGS):
                d = s[4 + a + lag, h : h + SUB, :] - here
                sums[n] += fold(d * d)
        for n, lag in enumerate(LAGS):
            inside = across is None or a + lag < ROWS
            acc[2 + n] += sums[n] if inside else sums[n] * across

    def h_copy(up):
        at, to, where = (4, 0, after) if up else (0, 4, before)
        n = 0 if up else 1
        return pltpu.make_async_remote_copy(
            hsend.at[pl.ds(at, 4)], hrecv.at[pl.ds(to, 4)], h_ssem.at[n], h_rsem.at[n],
            device_id=where, device_id_type=MESH,
        )

    add_row(12, first=True)

    @pl.loop(13, 16)
    def _(r):
        add_row(r)

    hsend[4:8] = s[16:20].astype(BF16)
    h_copy(True).start()

    @pl.loop(0, 4)
    def _(r):
        add_row(r)

    hsend[0:4] = s[4:8].astype(BF16)
    h_copy(False).start()

    @pl.loop(4, 11)
    def _(r):
        add_row(r)
        add_lags(r - 4)

    h_copy(False).wait_recv()
    s[20:24] = hrecv[4:8].astype(F32)
    inner = jnp.where(strip == STRIPS - 1, 0.0, 1.0).astype(F32)
    for a in range(12, 16):
        add_lags(a, inner)
    add_row(11)

    @pl.loop(7, 12)
    def _(a):
        add_lags(a)

    count = float(ROWS * HALF)
    drift = jnp.sum(acc[0], axis=0, keepdims=True) * (1.0 / count)
    tile[0:1] = mu[0:1, :] + drift
    tile[1:2] = jnp.sum(acc[1], axis=0, keepdims=True) - count * drift * drift
    for n in range(4):
        tile[2 + n : 3 + n] = jnp.sum(acc[2 + n], axis=0, keepdims=True)
    tile[6:8] = jnp.zeros((2, K), F32)

    def gather(size, me, peer, slots, send, recv):
        slots[me] = tile[...]

        def copy(j):
            return pltpu.make_async_remote_copy(
                tile, slots.at[me], send.at[j], recv.at[me],
                device_id=peer(j), device_id_type=MESH,
            )

        def arrival(j):
            slot = (me + j) % size
            return pltpu.make_async_remote_copy(
                tile, slots.at[slot], send.at[j], recv.at[slot],
                device_id=peer(j), device_id_type=MESH,
            )

        @pl.loop(1, size)
        def _(j):
            copy(j).start()

        @pl.loop(1, size)
        def _(j):
            arrival(j).wait_recv()

        @pl.loop(1, size)
        def _(j):
            copy(j).wait_send()

    def merge(slots, size, each):
        parts = [slots[n] for n in range(size)]
        total = parts[0]
        for part_ in parts[1:]:
            total = total + part_
        mean = total[0:1] * (1.0 / size)
        spread = jnp.zeros((1, K), F32)
        for part_ in parts:
            gap = part_[0:1] - mean
            spread += gap * gap
        return mean, total[1:2] + each * spread, total[2:6]

    gather(8, q, zc_peer, mom_a, ma_ssem, ma_rsem)
    mean, squares, lags = merge(mom_a, 8, count)
    tile[0:1] = mean
    tile[1:2] = squares
    tile[2:6] = lags
    gather(16, t, xy_peer, mom_b, mb_ssem, mb_rsem)
    mean, squares, lags = merge(mom_b, 16, 8 * count)
    cov = jnp.sum(squares, axis=1, keepdims=True) * (1.0 / NPIX)
    variogram = jnp.zeros((1, 1), F32)
    for n in range(4):
        variogram += jnp.sum(lags[n : n + 1], axis=1, keepdims=True) / (2.0 * PAIRS[n])
    objective = variogram / cov
    obj_out[0] = objective[0, 0]
    alpha = [jnp.broadcast_to((NPIX / n) / cov, (1, K)) for n in PAIRS]
    beta = jnp.broadcast_to(2.0 * objective / cov, (1, K))

    h_copy(True).wait_recv()
    s[0:4] = hrecv[0:4].astype(F32)

    def w_copy(r):
        return pltpu.make_async_remote_copy(
            w.at[r], wrecv.at[r], w_ssem.at[r], w_rsem.at[r],
            device_id=partner, device_id_type=MESH,
        )

    @pl.loop(0, ROWS)
    def _(r):
        row = strip * ROWS + r
        back = [alpha[n] * jnp.where(row >= lag, 1.0, 0.0) for n, lag in enumerate(LAGS)]
        ahead = [alpha[n] * jnp.where(row + lag < H, 1.0, 0.0) for n, lag in enumerate(LAGS)]
        for h in range(0, HALF, SUB):
            here = s[4 + r, h : h + SUB, :]
            value = beta * (mean - here)
            for n, lag in enumerate(LAGS):
                value += back[n] * (here - s[4 + r - lag, h : h + SUB, :])
                value += ahead[n] * (here - s[4 + r + lag, h : h + SUB, :])
            w[r, h : h + SUB, :] = value.astype(BF16)
        w_copy(r).start()

    grad[...] = jnp.zeros_like(grad)

    def add_grad(weights, data):
        grad[...] += lax.dot_general(
            weights, data, (((0,), (0,)), ((), ())), preferred_element_type=F32
        )

    @pl.loop(0, ROWS)
    def _(r):
        add_grad(w[r], xv[r, pl.ds(mine, HALF), :])

    @pl.loop(0, ROWS)
    def _(r):
        w_copy(r).wait_recv()
        add_grad(wrecv[r], xv[r, pl.ds(theirs, HALF), :])

    def z_copy(j, slot):
        return pltpu.make_async_remote_copy(
            grad.at[pl.ds(pl.multiple_of((q + j) % 8 * 8, 8), 8)], red_z.at[slot],
            z_ssem.at[j], z_rsem.at[slot], device_id=zc_peer(j), device_id_type=MESH,
        )

    def xx_copy(j, slot):
        return pltpu.make_async_remote_copy(
            grad.at[pl.ds(pl.multiple_of(64 + (u + j) % 8 * 8, 8), 8)], red_x.at[slot],
            xx_ssem.at[j], xx_rsem.at[slot], device_id=xc_peer(j), device_id_type=MESH,
        )

    @pl.loop(1, 8)
    def _(j):
        z_copy(j, q).start()
        xx_copy(j, u).start()

    red_z[q] = grad[pl.ds(pl.multiple_of(q * 8, 8), 8), :]
    red_x[u] = grad[pl.ds(pl.multiple_of(64 + u * 8, 8), 8), :]

    @pl.loop(1, 8)
    def _(j):
        z_copy(j, (q + j) % 8).wait_recv()
        xx_copy(j, (u + j) % 8).wait_recv()

    total_z, total_x = red_z[0], red_x[0]
    for n in range(1, 8):
        total_z = total_z + red_z[n]
        total_x = total_x + red_x[n]
    for n in range(4):
        part[n] = total_z[2 * n : 2 * n + 2, :]
        part[4 + n] = total_x[2 * n : 2 * n + 2, :]

    def bz_copy(j):
        to = (xx + j) % 4
        return pltpu.make_async_remote_copy(
            part.at[to], red_b.at[xx * 2 + ylo], b_ssem.at[j], b_rsem.at[xx * 2 + ylo],
            device_id=device_of(to, chan * 2, z, core), device_id_type=MESH,
        )

    def bx_copy(j):
        to = (z + j) % 4
        return pltpu.make_async_remote_copy(
            part.at[4 + to], red_b.at[z * 2 + ylo], b_ssem.at[4 + j], b_rsem.at[z * 2 + ylo],
            device_id=device_of(xx, chan * 2 + 1, to, core), device_id_type=MESH,
        )

    @pl.when(ylo == 0)
    def _():
        bx_copy(0).start()
        red_b[xx * 2] = part[xx]

    @pl.when(ylo == 1)
    def _():
        bz_copy(0).start()
        red_b[z * 2 + 1] = part[4 + z]

    for j in range(1, 4):
        bz_copy(j).start()
        bx_copy(j).start()
    own = jnp.where(ylo == 0, xx * 2, z * 2 + 1)

    @pl.loop(1, 8)
    def _(j):
        slot = (own + j) % 8
        pltpu.make_async_remote_copy(
            part.at[0], red_b.at[slot], b_ssem.at[0], b_rsem.at[slot],
            device_id=partner, device_id_type=MESH,
        ).wait_recv()

    total = red_b[0]
    for n in range(1, 8):
        total = total + red_b[n]
    g_out[...] = total

    @pl.loop(0, ROWS)
    def _(r):
        p_copy(r).wait_send()
        w_copy(r).wait_send()

    h_copy(True).wait_send()
    h_copy(False).wait_send()

    @pl.loop(1, 8)
    def _(j):
        z_copy(j, q).wait_send()
        xx_copy(j, u).wait_send()

    @pl.when(ylo == 0)
    def _():
        bx_copy(0).wait_send()

    @pl.when(ylo == 1)
    def _():
        bz_copy(0).wait_send()

    for j in range(1, 4):
        bz_copy(j).wait_send()
        bx_copy(j).wait_send()


def on_device(spectra, factors):
    dma = pltpu.SemaphoreType.DMA
    return pl.pallas_call(
        kernel,
        name="autocorrelation_gradient",
        out_shape=(
            jax.ShapeDtypeStruct((2, CH), F32),
            jax.ShapeDtypeStruct((1,), F32),
        ),
        in_specs=[pl.BlockSpec(memory_space=pl.ANY)] * 2,
        out_specs=(
            pl.BlockSpec(memory_space=pltpu.VMEM),
            pl.BlockSpec(memory_space=pltpu.SMEM),
        ),
        scratch_shapes=[
            pltpu.VMEM((ROWS, WP, CH), BF16),
            pltpu.VMEM((CH, K), BF16),
            pltpu.VMEM((CH, K), BF16),
            pltpu.VMEM((ROWS + 8, HALF, K), F32),
            pltpu.VMEM((ROWS, HALF, K), BF16),
            pltpu.VMEM((ROWS, HALF, K), BF16),
            pltpu.VMEM((8, HALF, K), BF16),
            pltpu.VMEM((8, HALF, K), BF16),
            pltpu.VMEM((ROWS, HALF, K), BF16),
            pltpu.VMEM((ROWS, HALF, K), BF16),
            pltpu.VMEM((8, K), F32),
            pltpu.VMEM((6, 8, K), F32),
            pltpu.VMEM((8, K), F32),
            pltpu.VMEM((8, 8, K), F32),
            pltpu.VMEM((16, 8, K), F32),
            pltpu.VMEM((K, CH), F32),
            pltpu.VMEM((8, 8, CH), F32),
            pltpu.VMEM((8, 8, CH), F32),
            pltpu.VMEM((8, 2, CH), F32),
            pltpu.VMEM((8, 2, CH), F32),
            dma((2 * ROWS,)),
            dma,
            dma((ROWS,)), dma((ROWS,)),
            dma((2,)), dma((2,)),
            dma((8,)), dma((8,)),
            dma((16,)), dma((16,)),
            dma((ROWS,)), dma((ROWS,)),
            dma((8,)), dma((8,)),
            dma((8,)), dma((8,)),
            dma((8,)), dma((8,)),
        ],
        compiler_params=pltpu.CompilerParams(
            collective_id=0, has_side_effects=True, vmem_limit_bytes=56 << 20
        ),
    )(spectra, factors)


def solution(mesh):
    return jax.shard_map(
        on_device,
        mesh=mesh,
        in_specs=(P("rows", None, "chan"), P("chan", None)),
        out_specs=(P("rows", "chan"), P()),
        check_vma=False,
    )
```

time: 1020 us -> 84.4 us (0.08)
  waiting for transfers between devices: 656 us -> 0 us
  blocking collectives: 281 us -> 0 us
  Pallas kernels: 0 us -> 80.5 us
  matrix products: 34.5 us -> 0 us
  between operations: 20.6 us -> 2.4 us
  other arithmetic: 11.9 us -> 0 us
    unnamed x3 -> x0, waiting for transfers between devices: 537 us -> none
    psum x2 -> x0, blocking collectives: 281 us -> none  [the longest x1 143 us: on_device(): moments = lax.psum(jnp.stack([centered_sq] + lag_terms), 'rows')]
    psum x1 -> x0, waiting for transfers between devices: 119 us -> none  [on_device(): scores = lax.psum(partial_scores, 'chan')]
    pallas_call x0 -> x1, Pallas kernels: none -> 80.5 us  [on_device(): pl.pallas_call(kernel, name='autocorrelation_gradient', out_shape=(jax.Sh...]
    dot_general x2 -> x0, matrix products: 34.5 us -> none  [the longest x1 24.3 us: on_device(): lax.dot_general(weight_rows, pixel_rows, (((0,), (0,)), ((), ())), prefer...]
    reduce_sum x4 -> x0, other arithmetic: 11.9 us -> none  [the longest x1 4.48 us: on_device(): lag_terms.append(jnp.sum(forward_diff * forward_diff, axis=(0, 1)))]
  transfers between devices with their start and end apart: 4 -> 0, of which waited for: 2 -> 0; matrix products, arithmetic and copies ran while one was open for 2% -> 0% of each run, Pallas kernels for 0% -> 0%
where the time goes in v1:
time: 84.4 us; the launch traced here: 84.2 us
  Pallas kernels  80.5 us (95%)
  between operations  2.4 us (3%)
  local copies, waits for them, and re-layouts  1.3 us (2%)
    pallas_call x1, Pallas kernels, on_device(): pl.pallas_call(kernel, name='autocorrelation_gradient', out_shape=(jax.Sh...  80.5 us

profile of v1, /device:TPU:1, one launch (start us, length us, event | category | flops | bytes accessed | tf_op | source)
XLA Modules:
  0.0 84.2 jit_solution(223350058749236711)
XLA Ops:
  0.6 80.5 %autocorrelation_gradient.1 = (f32[2,1024]{1,0:T(2,128)}, f32[1]{0:T(128)}) custom-call(bf16[16,512,1024]{2,1,0:T(8,128)(2,1)} %x_hbm.1, bf16[1024,128]{1,0:T(8,128)(2,1)} %f_hbm.1), custom_call_target="tpu_custom_call" | custom-call | tf_op jit(solution)/shard_map/autocorrelation_gradient/pallas_call | solution.py:416
  81.2 1.3 %copy.6 = f32[2,1024]{1,0:T(2,128)} copy(f32[2,1024]{1,0:T(2,128)} %get-tuple-element.4) | data formatting | bytes 16384

commit v2 on v1

v2 whole, which is shorter than its diff:
```python
import jax
import jax.numpy as jnp
from jax import lax
from jax.experimental import pallas as pl
from jax.experimental.pallas import tpu as pltpu
from jax.sharding import PartitionSpec as P

MESH = pl.DeviceIdType.MESH
F32, BF16 = jnp.float32, jnp.bfloat16

ROWS = 16
STRIPS = 64
WP = 512
HALF = 256
EXT = 128
REST = HALF - EXT
K = 128
CH = 1024
H = ROWS * STRIPS
NPIX = float(H * WP)
LAGS = (1, 2, 3, 4)
PAIRS = tuple(float((H - lag) * WP) for lag in LAGS)
AHEAD = 4
FLYING = 8
GOING = 4
SUB = 32


def device_of(x, y, z, core):
    return ((x * 2 + y % 2) * 4 + z) * 2 + core, y // 2


def fold(block):
    return jnp.sum(block.reshape(block.shape[0] // 8, 8, K), axis=0)


def kernel(
    x_hbm, f_hbm, g_out, obj_out,
    xo, xe, xt, fv, fp, s, se, psend, precv, pxsend, pxrecv, hsend, hrecv, hxsend, hxrecv,
    w, we, wrecv, mu, acc, tile, tile_b, mom_a, mom_b, grad,
    red_z, red_x, part, red_b,
    x_sem, f_sem, p_ssem, p_rsem, px_ssem, px_rsem, h_ssem, h_rsem, hx_ssem, hx_rsem, ma_ssem, ma_rsem, mb_ssem, mb_rsem,
    w_ssem, w_rsem, z_ssem, z_rsem, xx_ssem, xx_rsem, b_ssem, b_rsem,
):
    strip = lax.axis_index("rows")
    chan = lax.axis_index("chan")
    core, z, ylo, xx = strip % 2, (strip // 2) % 4, (strip // 8) % 2, strip // 16
    y = chan * 2 + ylo
    mine = pl.multiple_of(chan * HALF, HALF)
    theirs = pl.multiple_of((1 - chan) * HALF, HALF)
    partner = (strip, 1 - chan)
    after = ((strip + 1) % STRIPS, chan)
    before = ((strip + STRIPS - 1) % STRIPS, chan)

    def order(i):
        return i // 4 * 12 % ROWS + i % 4

    def x_copy(r, n):
        at, size, to = ((theirs, EXT, xe), (theirs + EXT, REST, xt), (mine, HALF, xo))[n]
        return pltpu.make_async_copy(
            x_hbm.at[r, pl.ds(pl.multiple_of(at, SUB), size), :],
            to.at[pl.ds(pl.multiple_of(r * size, SUB), size), :],
            x_sem.at[n, r],
        )

    f_copy = pltpu.make_async_copy(f_hbm, fv, f_sem)
    f_copy.start()

    for i in range(AHEAD):
        x_copy(order(i), 0).start()
        x_copy(order(i), 1).start()

    barrier = pltpu.get_barrier_semaphore()

    def greet(place):
        pl.semaphore_signal(barrier, inc=1, device_id=place, device_id_type=MESH)

    q = z * 2 + core
    t = xx * 4 + y
    u = xx * 2 + core

    def zc_peer(j):
        other = (q + j) % 8
        return device_of(xx, y, other // 2, other % 2)

    def xy_peer(j):
        other = (t + j) % 16
        return device_of(other // 4, other % 4, z, core)

    def xc_peer(j):
        other = (u + j) % 8
        return device_of(other // 2, y, z, other % 2)

    @pl.loop(1, 8)
    def _(j):
        greet(zc_peer(j))

    @pl.loop(1, 16)
    def _(j):
        greet(xy_peer(j))

    @pl.loop(1, 4)
    def _(j):
        greet(device_of((xx + j) % 4, y, z, 1 - core))
        greet(device_of(xx, chan * 2 + 1 - ylo, (z + j) % 4, core))

    greet(after)
    greet(before)
    greet(device_of((xx + 1) % 4, y, 3 - z, 1 - core))
    greet(device_of((xx + 3) % 4, y, 3 - z, 1 - core))

    f_copy.wait()
    src = lax.broadcasted_iota(jnp.int32, (K, K), 0)
    dst = lax.broadcasted_iota(jnp.int32, (K, K), 1)
    hi, mid, lo, e = dst >> 6, (dst >> 3) & 7, (dst >> 1) & 3, dst & 1
    to_x = jnp.where(hi == 0, lo, mid >> 1)
    to_z = jnp.where(hi == 0, mid >> 1, lo)
    from_k = (((to_x * 2 + hi) * 4 + to_z) * 2 + (mid & 1)) * 2 + e
    permutation = jnp.where(src == from_k, 1.0, 0.0).astype(BF16)
    fp[...] = jnp.dot(fv[...], permutation, preferred_element_type=F32).astype(BF16)

    def p_copy(r):
        return pltpu.make_async_remote_copy(
            psend.at[r], precv.at[r], p_ssem.at[r], p_rsem.at[r],
            device_id=partner, device_id_type=MESH,
        )

    def scores(ref, r, size):
        data = ref[pl.ds(pl.multiple_of(r * size, SUB), size), :]
        return jnp.dot(data, fp[...], preferred_element_type=F32)

    @pl.loop(0, ROWS)
    def _(i):
        r = order(i)

        @pl.when(i + AHEAD < ROWS)
        def _():
            x_copy(order(i + AHEAD), 0).start()
            x_copy(order(i + AHEAD), 1).start()

        x_copy(r, 2).start()
        x_copy(r, 0).wait()
        psend[r, 0:EXT, :] = scores(xe, r, EXT).astype(BF16)
        x_copy(r, 1).wait()
        psend[r, EXT:HALF, :] = scores(xt, r, REST).astype(BF16)

        @pl.when(i == 0)
        def _():
            pl.semaphore_wait(barrier, 32)

        @pl.when(i < FLYING)
        def _():
            p_copy(r).start()

    acc[...] = jnp.zeros_like(acc)

    def add_row(i, first=False):
        r = order(i)
        p_copy(r).wait_send()

        @pl.when(i + FLYING < ROWS)
        def _():
            p_copy(order(i + FLYING)).start()

        x_copy(r, 2).wait()
        s[4 + r] = scores(xo, r, HALF)
        pxsend[r] = s[4 + r, 0:EXT, :].astype(BF16)
        p_copy(r).wait_recv()
        if first:
            total = jnp.zeros((8, K), F32)
            for h in range(0, HALF, SUB):
                total += fold(s[4 + r, h : h + SUB, :] + precv[r, h : h + SUB, :].astype(F32))
            mu[...] = jnp.broadcast_to(
                jnp.sum(total, axis=0, keepdims=True) * (1.0 / HALF), (8, K)
            )
        shift = mu[0:1, :]
        one, two = jnp.zeros((8, K), F32), jnp.zeros((8, K), F32)
        for h in range(0, HALF, SUB):
            v = s[4 + r, h : h + SUB, :] + precv[r, h : h + SUB, :].astype(F32)
            s[4 + r, h : h + SUB, :] = v
            d = v - shift
            one += fold(d)
            two += fold(d * d)
        acc[0] += one
        acc[1] += two

    def add_lags(a, across=None):
        sums = [jnp.zeros((8, K), F32) for _ in LAGS]
        for h in range(0, HALF, SUB):
            here = s[4 + a, h : h + SUB, :]
            for n, lag in enumerate(LAGS):
                d = s[4 + a + lag, h : h + SUB, :] - here
                sums[n] += fold(d * d)
        for n, lag in enumerate(LAGS):
            inside = across is None or a + lag < ROWS
            acc[2 + n] += sums[n] if inside else sums[n] * across

    class Halo:
        def __init__(self, size, send, hold, send_sem, recv_sem):
            self.size, self.send, self.hold, self.sems = size, send, hold, (send_sem, recv_sem)

        def copy(self, up, n, hop, source, slot, place):
            way = 0 if up else 1
            return pltpu.make_async_remote_copy(
                source, self.held(up, n, slot),
                self.sems[0].at[way, hop, n], self.sems[1].at[way, slot, n],
                device_id=place, device_id_type=MESH,
            )

        def held(self, up, n, slot):
            return self.hold.at[slot, pl.ds((0 if up else 4) + n * self.size, self.size)]

        def first(self, up, n, far=False):
            source = self.send.at[pl.ds((4 if up else 0) + n * self.size, self.size)]
            if far and (not up or self.size == 4):
                return self.copy(up, n, 0, source, 0, after if up else before)
            if far:
                return self.copy(up, n, 0, source, 1, device_of(xx, chan * 2 + 1 - ylo, z, core))
            return self.copy(up, n, 0, source, 0, zc_peer(1 if up else 7))

        def second(self, n):
            place = device_of((xx + 1 - ylo) % 4, y, 0, 0)
            return self.copy(True, n, 1, self.held(True, n, 1), 0, place)

        def end(self, up):
            return (z == 3) & (core == 1) if up else (z == 0) & (core == 0)

        def start(self, up, n=0):
            @pl.when(self.end(up))
            def _():
                self.first(up, n, far=True).start()

            @pl.when(jnp.logical_not(self.end(up)))
            def _():
                self.first(up, n).start()

        def arrive(self, up, n=0, slot=0):
            self.copy(up, n, 0, self.held(up, n, slot), slot, partner).wait_recv()

        def relay(self, n=0):
            @pl.when(self.end(True))
            def _():
                self.arrive(True, n, 1)
                self.second(n).start()

        def drain(self, up):
            @pl.loop(0, 4 // self.size)
            def _(n):
                self.first(up, n).wait_send()
                if not up or self.size == 4:
                    return

                @pl.when(self.end(up))
                def _():
                    self.second(n).wait_send()

    halo = Halo(1, hsend, hrecv, h_ssem, h_rsem)
    halo_ext = Halo(4, hxsend, hxrecv, hx_ssem, hx_rsem)
    UP, DOWN = True, False

    def px_copy(n):
        return pltpu.make_async_remote_copy(
            pxsend.at[pl.ds(n * 4, 4)], pxrecv.at[pl.ds(n * 4, 4)], px_ssem.at[n], px_rsem.at[n],
            device_id=partner, device_id_type=MESH,
        )

    def send_down(n):
        hsend[n] = s[4 + n].astype(BF16)
        halo.start(DOWN, n)

    add_row(0, first=True)
    send_down(0)

    @pl.loop(1, 4)
    def _(n):
        add_row(n)
        send_down(n)

    @pl.loop(0, 4)
    def _(n):
        add_row(4 + n)
        hsend[4 + n] = s[16 + n].astype(BF16)
        halo.start(UP, n)

    @pl.loop(0, 4)
    def _(n):
        add_row(8 + n)

    @pl.loop(8, 12)
    def _(a):
        add_lags(a)

    @pl.loop(0, 3)
    def _(n):
        add_row(12 + n)
        add_lags(n)

    px_copy(0).start()
    for n in range(4):
        halo.arrive(DOWN, n)
    s[20:24] = hrecv[0, 4:8].astype(F32)
    inner = jnp.where(strip == STRIPS - 1, 0.0, 1.0).astype(F32)
    for a in range(12, 16):
        add_lags(a, inner)
    add_row(15)
    px_copy(3).start()

    @pl.loop(3, 8)
    def _(a):
        add_lags(a)

    count = float(ROWS * HALF)
    drift = jnp.sum(acc[0], axis=0, keepdims=True) * (1.0 / count)
    tile[0:1] = mu[0:1, :] + drift
    tile[1:2] = jnp.sum(acc[1], axis=0, keepdims=True) - count * drift * drift
    for n in range(4):
        tile[2 + n : 3 + n] = jnp.sum(acc[2 + n], axis=0, keepdims=True)
    tile[6:8] = jnp.zeros((2, K), F32)

    def gather(tile, size, me, peer, slots, send, recv, beside):
        slots[me] = tile[...]

        def copies(source, target, place):
            return pltpu.make_async_remote_copy(
                source, target, send, recv, device_id=place, device_id_type=MESH
            )

        @pl.loop(1, size)
        def _(j):
            copies(tile, slots.at[me], peer(j)).start()

        px_copy(beside).start()
        others = slots.at[pl.ds(0, size - 1)]
        copies(others, others, partner).wait_recv()
        return copies(others, others, partner)

    def merge(slots, size, each):
        parts = [slots[n] for n in range(size)]
        total = parts[0]
        for part_ in parts[1:]:
            total = total + part_
        mean = total[0:1] * (1.0 / size)
        spread = jnp.zeros((1, K), F32)
        for part_ in parts:
            gap = part_[0:1] - mean
            spread += gap * gap
        return mean, total[1:2] + each * spread, total[2:6]

    sent_a = gather(tile, 8, q, zc_peer, mom_a, ma_ssem, ma_rsem, 2)
    mean, squares, lags = merge(mom_a, 8, count)
    tile_b[0:1] = mean
    tile_b[1:2] = squares
    tile_b[2:6] = lags
    tile_b[6:8] = jnp.zeros((2, K), F32)
    sent_b = gather(tile_b, 16, t, xy_peer, mom_b, mb_ssem, mb_rsem, 1)
    mean, squares, lags = merge(mom_b, 16, 8 * count)
    cov = jnp.sum(squares, axis=1, keepdims=True) * (1.0 / NPIX)
    variogram = jnp.zeros((1, 1), F32)
    for n in range(4):
        variogram += jnp.sum(lags[n : n + 1], axis=1, keepdims=True) / (2.0 * PAIRS[n])
    objective = variogram / cov
    obj_out[0] = objective[0, 0]
    alpha = [jnp.broadcast_to((NPIX / n) / cov, (1, K)) for n in PAIRS]
    beta = jnp.broadcast_to(2.0 * objective / cov, (1, K))

    for n in range(4):
        halo.relay(n)

    def w_copy(r):
        return pltpu.make_async_remote_copy(
            w.at[pl.ds(pl.multiple_of(r * HALF + EXT, SUB), REST)],
            wrecv.at[pl.ds(pl.multiple_of(r * REST, SUB), REST)], w_ssem.at[r], w_rsem.at[r],
            device_id=partner, device_id_type=MESH,
        )

    def weigh(r, source, target, size):
        row = strip * ROWS + r
        back = [alpha[n] * jnp.where(row >= lag, 1.0, 0.0) for n, lag in enumerate(LAGS)]
        ahead = [alpha[n] * jnp.where(row + lag < H, 1.0, 0.0) for n, lag in enumerate(LAGS)]
        for h in range(0, size, SUB):
            here = source[4 + r, h : h + SUB, :]
            value = beta * (mean - here)
            for n, lag in enumerate(LAGS):
                value += back[n] * (here - source[4 + r - lag, h : h + SUB, :])
                value += ahead[n] * (here - source[4 + r + lag, h : h + SUB, :])
            target[pl.ds(pl.multiple_of(r * size + h, SUB), SUB), :] = value.astype(BF16)

    def go(k):
        w_copy((k + 4) % ROWS).start()

    def tick(k):
        w_copy((k + 4) % ROWS).wait_send()
        go(k + GOING)

    @pl.loop(0, 8)
    def _(k):
        weigh(k + 4, s, w, HALF)

        @pl.when(k < GOING)
        def _():
            go(k)

    for n in range(4):
        halo.arrive(UP, n)
    s[0:4] = hrecv[0, 0:4].astype(F32)

    @pl.loop(0, 4)
    def _(n):
        weigh(12 + n, s, w, HALF)
        tick(n)

    pl.loop(0, 4)(lambda n: weigh(n, s, w, HALF))

    for n in range(4):
        px_copy(n).wait_recv()

    @pl.loop(0, ROWS)
    def _(r):
        se[4 + r] = psend[r, 0:EXT, :].astype(F32) + pxrecv[r].astype(F32)

    hxsend[0:4] = se[4:8].astype(BF16)
    hxsend[4:8] = se[16:20].astype(BF16)
    halo_ext.start(DOWN)
    halo_ext.start(UP)
    grad[...] = jnp.zeros_like(grad)

    def add_grad(weights, data):
        grad[...] += lax.dot_general(
            weights, data, (((0,), (0,)), ((), ())), preferred_element_type=F32
        )

    def own_grad(n):
        some = pl.ds(pl.multiple_of(n * CH, CH), CH)
        add_grad(w[some, :], xo[some, :])

    def rest_grad(start, rows):
        for r in range(start, start + rows):
            w_copy(r).wait_recv()
        some = slice(start * REST, (start + rows) * REST)
        add_grad(wrecv[some, :], xt[some, :])

    @pl.loop(0, 2)
    def _(n):
        own_grad(n)
        tick(4 + n)

    @pl.loop(2, 4)
    def _(n):
        own_grad(n)
        tick(4 + n)

    rest_grad(4, 4)
    tick(8)
    tick(9)
    tick(10)
    tick(11)
    rest_grad(8, 4)
    halo_ext.arrive(DOWN)
    halo_ext.arrive(UP)
    se[20:24] = hxrecv[0, 4:8].astype(F32)
    se[0:4] = hxrecv[0, 0:4].astype(F32)

    @pl.loop(0, ROWS)
    def _(r):
        weigh(r, se, we, EXT)

    add_grad(we[...], xe[...])
    for start, rows in ((12, 4), (0, 2), (2, 1), (3, 1)):
        rest_grad(start, rows)

    def z_copy(j):
        return pltpu.make_async_remote_copy(
            grad.at[pl.ds(pl.multiple_of((q + j) % 8 * 8, 8), 8)], red_z.at[q],
            z_ssem, z_rsem, device_id=zc_peer(j), device_id_type=MESH,
        )

    def xx_copy(j):
        return pltpu.make_async_remote_copy(
            grad.at[pl.ds(pl.multiple_of(64 + (u + j) % 8 * 8, 8), 8)], red_x.at[u],
            xx_ssem, xx_rsem, device_id=xc_peer(j), device_id_type=MESH,
        )

    def seven(ref, send, recv):
        some = ref.at[pl.ds(0, 7)]
        return pltpu.make_async_remote_copy(
            some, some, send, recv, device_id=partner, device_id_type=MESH
        )

    @pl.loop(1, 8)
    def _(j):
        z_copy(j).start()
        xx_copy(j).start()

    red_z[q] = grad[pl.ds(pl.multiple_of(q * 8, 8), 8), :]
    red_x[u] = grad[pl.ds(pl.multiple_of(64 + u * 8, 8), 8), :]

    seven(red_z, z_ssem, z_rsem).wait_recv()
    seven(red_x, xx_ssem, xx_rsem).wait_recv()
    total_z, total_x = red_z[0], red_x[0]
    for n in range(1, 8):
        total_z = total_z + red_z[n]
        total_x = total_x + red_x[n]
    for n in range(4):
        part[n] = total_z[2 * n : 2 * n + 2, :]
        part[4 + n] = total_x[2 * n : 2 * n + 2, :]

    def bz_copy(j):
        to = (xx + j) % 4
        return pltpu.make_async_remote_copy(
            part.at[to], red_b.at[xx * 2 + ylo], b_ssem, b_rsem,
            device_id=device_of(to, chan * 2, z, core), device_id_type=MESH,
        )

    def bx_copy(j):
        to = (z + j) % 4
        return pltpu.make_async_remote_copy(
            part.at[4 + to], red_b.at[z * 2 + ylo], b_ssem, b_rsem,
            device_id=device_of(xx, chan * 2 + 1, to, core), device_id_type=MESH,
        )

    @pl.when(ylo == 0)
    def _():
        bx_copy(0).start()
        red_b[xx * 2] = part[xx]

    @pl.when(ylo == 1)
    def _():
        bz_copy(0).start()
        red_b[z * 2 + 1] = part[4 + z]

    for j in range(1, 4):
        bz_copy(j).start()
        bx_copy(j).start()
    seven(red_b, b_ssem, b_rsem).wait_recv()
    total = red_b[0]
    for n in range(1, 8):
        total = total + red_b[n]
    g_out[...] = total

    sent_a.wait_send()
    sent_b.wait_send()

    @pl.loop(0, 4)
    def _(r):
        w_copy(r).wait_send()

    for n in range(4):
        px_copy(n).wait_send()
    for up in (False, True):
        halo.drain(up)
        halo_ext.drain(up)

    seven(red_z, z_ssem, z_rsem).wait_send()
    seven(red_x, xx_ssem, xx_rsem).wait_send()
    seven(red_b, b_ssem, b_rsem).wait_send()


def on_device(spectra, factors):
    dma = pltpu.SemaphoreType.DMA
    return pl.pallas_call(
        kernel,
        name="autocorrelation_gradient",
        out_shape=(
            jax.ShapeDtypeStruct((2, CH), F32),
            jax.ShapeDtypeStruct((1,), F32),
        ),
        in_specs=[pl.BlockSpec(memory_space=pl.ANY)] * 2,
        out_specs=(
            pl.BlockSpec(memory_space=pltpu.VMEM),
            pl.BlockSpec(memory_space=pltpu.SMEM),
        ),
        scratch_shapes=[
            pltpu.VMEM((ROWS * HALF, CH), BF16),
            pltpu.VMEM((ROWS * EXT, CH), BF16),
            pltpu.VMEM((ROWS * REST, CH), BF16),
            pltpu.VMEM((CH, K), BF16),
            pltpu.VMEM((CH, K), BF16),
            pltpu.VMEM((ROWS + 8, HALF, K), F32),
            pltpu.VMEM((ROWS + 8, EXT, K), F32),
            pltpu.VMEM((ROWS, HALF, K), BF16),
            pltpu.VMEM((ROWS, HALF, K), BF16),
            pltpu.VMEM((ROWS, EXT, K), BF16),
            pltpu.VMEM((ROWS, EXT, K), BF16),
            pltpu.VMEM((8, HALF, K), BF16),
            pltpu.VMEM((2, 8, HALF, K), BF16),
            pltpu.VMEM((8, EXT, K), BF16),
            pltpu.VMEM((2, 8, EXT, K), BF16),
            pltpu.VMEM((ROWS * HALF, K), BF16),
            pltpu.VMEM((ROWS * EXT, K), BF16),
            pltpu.VMEM((ROWS * REST, K), BF16),
            pltpu.VMEM((8, K), F32),
            pltpu.VMEM((6, 8, K), F32),
            pltpu.VMEM((8, K), F32),
            pltpu.VMEM((8, K), F32),
            pltpu.VMEM((8, 8, K), F32),
            pltpu.VMEM((16, 8, K), F32),
            pltpu.VMEM((K, CH), F32),
            pltpu.VMEM((8, 8, CH), F32),
            pltpu.VMEM((8, 8, CH), F32),
            pltpu.VMEM((8, 2, CH), F32),
            pltpu.VMEM((8, 2, CH), F32),
            dma((3, ROWS)),
            dma,
            dma((ROWS,)), dma((ROWS,)),
            dma((4,)), dma((4,)),
            dma((2, 2, 4)), dma((2, 2, 4)),
            dma((2, 2, 1)), dma((2, 2, 1)),
            dma, dma,
            dma, dma,
            dma((ROWS,)), dma((ROWS,)),
            dma, dma,
            dma, dma,
            dma, dma,
        ],
        compiler_params=pltpu.CompilerParams(
            collective_id=0, has_side_effects=True, vmem_limit_bytes=56 << 20
        ),
    )(spectra, factors)


def solution(mesh):
    return jax.shard_map(
        on_device,
        mesh=mesh,
        in_specs=(P("rows", None, "chan"), P("chan", None)),
        out_specs=(P("rows", "chan"), P()),
        check_vma=False,
    )
```

time: 84.4 us -> 76.9 us (0.911)
  Pallas kernels: 80.5 us -> 73 us
    pallas_call x1, Pallas kernels: 80.5 us -> 73 us  [on_device(): pl.pallas_call(kernel, name='autocorrelation_gradient', out_shape=(jax.Sh...]
where the time goes in v2:
time: 76.9 us; the launch traced here: 76.7 us
  Pallas kernels  73 us (95%)
  between operations  2.4 us (3%)
  local copies, waits for them, and re-layouts  1.3 us (2%)
    pallas_call x1, Pallas kernels, on_device(): pl.pallas_call(kernel, name='autocorrelation_gradient', out_shape=(jax.Sh...  73 us

profile of v2, /device:TPU:1, one launch (start us, length us, event | category | flops | bytes accessed | tf_op | source)
XLA Modules:
  0.0 76.7 jit_solution(7906571737440240953)
XLA Ops:
  0.6 73.0 %autocorrelation_gradient.1 = (f32[2,1024]{1,0:T(2,128)}, f32[1]{0:T(128)}) custom-call(bf16[16,512,1024]{2,1,0:T(8,128)(2,1)} %x_hbm.1, bf16[1024,128]{1,0:T(8,128)(2,1)} %f_hbm.1), custom_call_target="tpu_custom_call" | custom-call | tf_op jit(solution)/shard_map/autocorrelation_gradient/pallas_call | solution.py:560
  73.6 1.3 %copy.6 = f32[2,1024]{1,0:T(2,128)} copy(f32[2,1024]{1,0:T(2,128)} %get-tuple-element.4) | data formatting | bytes 16384

commit v3 on v2

--- a/solution.py
+++ b/solution.py
@@ -22,7 +22,7 @@
 PAIRS = tuple(float((H - lag) * WP) for lag in LAGS)
 AHEAD = 4
 FLYING = 8
-GOING = 4
+GOING = 6
 SUB = 32
 
 
@@ -38,9 +38,10 @@
     x_hbm, f_hbm, g_out, obj_out,
     xo, xe, xt, fv, fp, s, se, psend, precv, pxsend, pxrecv, hsend, hrecv, hxsend, hxrecv,
     w, we, wrecv, mu, acc, tile, tile_b, mom_a, mom_b, grad,
-    red_z, red_x, part, red_b,
+    red_z, red_x, part, red_b, late, piece, late_z, late_x,
     x_sem, f_sem, p_ssem, p_rsem, px_ssem, px_rsem, h_ssem, h_rsem, hx_ssem, hx_rsem, ma_ssem, ma_rsem, mb_ssem, mb_rsem,
     w_ssem, w_rsem, z_ssem, z_rsem, xx_ssem, xx_rsem, b_ssem, b_rsem,
+    lz_ssem, lz_rsem, lx_ssem, lx_rsem,
 ):
     strip = lax.axis_index("rows")
     chan = lax.axis_index("chan")
@@ -390,7 +391,11 @@
 
     def tick(k):
         w_copy((k + 4) % ROWS).wait_send()
-        go(k + GOING)
+        if isinstance(k, int):
+            if k + GOING < ROWS:
+                go(k + GOING)
+        else:
+            pl.when(k + GOING < ROWS)(lambda: go(k + GOING))
 
     @pl.loop(0, 8)
     def _(k):
@@ -424,8 +429,8 @@
     halo_ext.start(UP)
     grad[...] = jnp.zeros_like(grad)
 
-    def add_grad(weights, data):
-        grad[...] += lax.dot_general(
+    def add_grad(weights, data, total=grad):
+        total[...] += lax.dot_general(
             weights, data, (((0,), (0,)), ((), ())), preferred_element_type=F32
         )
 
@@ -433,11 +438,11 @@
         some = pl.ds(pl.multiple_of(n * CH, CH), CH)
         add_grad(w[some, :], xo[some, :])
 
-    def rest_grad(start, rows):
+    def rest_grad(start, rows, total=grad):
         for r in range(start, start + rows):
             w_copy(r).wait_recv()
         some = slice(start * REST, (start + rows) * REST)
-        add_grad(wrecv[some, :], xt[some, :])
+        add_grad(wrecv[some, :], xt[some, :], total)
 
     @pl.loop(0, 2)
     def _(n):
@@ -465,9 +470,6 @@
         weigh(r, se, we, EXT)
 
     add_grad(we[...], xe[...])
-    for start, rows in ((12, 4), (0, 2), (2, 1), (3, 1)):
-        rest_grad(start, rows)
-
     def z_copy(j):
         return pltpu.make_async_remote_copy(
             grad.at[pl.ds(pl.multiple_of((q + j) % 8 * 8, 8), 8)], red_z.at[q],
@@ -491,6 +493,33 @@
         z_copy(j).start()
         xx_copy(j).start()
 
+    late[...] = jnp.zeros_like(late)
+    for start, rows in ((12, 4), (0, 2), (2, 1), (3, 1)):
+        rest_grad(start, rows, late)
+
+    for n in range(16):
+        term = late[8 * n : 8 * n + 8, :]
+        piece[n] = jnp.concatenate([term[:, :512], term[:, 512:]], axis=0).astype(BF16)
+
+    def lz_copy(j):
+        return pltpu.make_async_remote_copy(
+            piece.at[(q + j) % 8], late_z.at[q], lz_ssem, lz_rsem,
+            device_id=zc_peer(j), device_id_type=MESH,
+        )
+
+    def lx_copy(j):
+        return pltpu.make_async_remote_copy(
+            piece.at[8 + (u + j) % 8], late_x.at[u], lx_ssem, lx_rsem,
+            device_id=xc_peer(j), device_id_type=MESH,
+        )
+
+    @pl.loop(1, 8)
+    def _(j):
+        lz_copy(j).start()
+        lx_copy(j).start()
+
+    late_z[q] = piece[q]
+    late_x[u] = piece[8 + u]
     red_z[q] = grad[pl.ds(pl.multiple_of(q * 8, 8), 8), :]
     red_x[u] = grad[pl.ds(pl.multiple_of(64 + u * 8, 8), 8), :]
 
@@ -500,6 +529,17 @@
     for n in range(1, 8):
         total_z = total_z + red_z[n]
         total_x = total_x + red_x[n]
+    seven(late_z, lz_ssem, lz_rsem).wait_recv()
+    seven(late_x, lx_ssem, lx_rsem).wait_recv()
+
+    def all_late(ref):
+        term = ref[0].astype(F32)
+        for n in range(1, 8):
+            term = term + ref[n].astype(F32)
+        return jnp.concatenate([term[0:8], term[8:16]], axis=1)
+
+    total_z = total_z + all_late(late_z)
+    total_x = total_x + all_late(late_x)
     for n in range(4):
         part[n] = total_z[2 * n : 2 * n + 2, :]
         part[4 + n] = total_x[2 * n : 2 * n + 2, :]
@@ -553,6 +593,8 @@
     seven(red_z, z_ssem, z_rsem).wait_send()
     seven(red_x, xx_ssem, xx_rsem).wait_send()
     seven(red_b, b_ssem, b_rsem).wait_send()
+    seven(late_z, lz_ssem, lz_rsem).wait_send()
+    seven(late_x, lx_ssem, lx_rsem).wait_send()
 
 
 def on_device(spectra, factors):
@@ -599,6 +641,10 @@
             pltpu.VMEM((8, 8, CH), F32),
             pltpu.VMEM((8, 2, CH), F32),
             pltpu.VMEM((8, 2, CH), F32),
+            pltpu.VMEM((K, CH), F32),
+            pltpu.VMEM((16, 16, CH // 2), BF16),
+            pltpu.VMEM((8, 16, CH // 2), BF16),
+            pltpu.VMEM((8, 16, CH // 2), BF16),
             dma((3, ROWS)),
             dma,
             dma((ROWS,)), dma((ROWS,)),
@@ -611,6 +657,8 @@
             dma, dma,
             dma, dma,
             dma, dma,
+            dma, dma,
+            dma, dma,
         ],
         compiler_params=pltpu.CompilerParams(
             collective_id=0, has_side_effects=True, vmem_limit_bytes=56 << 20

time: 76.9 us -> 76.2 us (level)
  no operation moved by 1% of the time
where the time goes in v3:
time: 76.2 us; the launch traced here: 76 us
  Pallas kernels  72.3 us (95%)
  between operations  2.4 us (3%)
  local copies, waits for them, and re-layouts  1.3 us (2%)
    pallas_call x1, Pallas kernels, on_device(): pl.pallas_call(kernel, name='autocorrelation_gradient', out_shape=(jax.Sh...  72.3 us

profile of v3, /device:TPU:1, one launch (start us, length us, event | category | flops | bytes accessed | tf_op | source)
XLA Modules:
  0.0 76.0 jit_solution(708101258018826312)
XLA Ops:
  0.6 72.3 %autocorrelation_gradient.1 = (f32[2,1024]{1,0:T(2,128)}, f32[1]{0:T(128)}) custom-call(bf16[16,512,1024]{2,1,0:T(8,128)(2,1)} %x_hbm.1, bf16[1024,128]{1,0:T(8,128)(2,1)} %f_hbm.1), custom_call_target="tpu_custom_call" | custom-call | tf_op jit(solution)/shard_map/autocorrelation_gradient/pallas_call | solution.py:602
  73.0 1.3 %copy.6 = f32[2,1024]{1,0:T(2,128)} copy(f32[2,1024]{1,0:T(2,128)} %get-tuple-element.4) | data formatting | bytes 16384

commit v4 on v3

--- a/solution.py
+++ b/solution.py
@@ -105,10 +105,17 @@
         greet(device_of((xx + j) % 4, y, z, 1 - core))
         greet(device_of(xx, chan * 2 + 1 - ylo, (z + j) % 4, core))
 
-    greet(after)
-    greet(before)
-    greet(device_of((xx + 1) % 4, y, 3 - z, 1 - core))
-    greet(device_of((xx + 3) % 4, y, 3 - z, 1 - core))
+    @pl.when((z == 3) & (core == 1))
+    def _():
+        greet(after)
+        greet(device_of((xx + 1) % 4, y, 0, 0))
+
+    @pl.when((z == 0) & (core == 0))
+    def _():
+        greet(before)
+        greet(device_of((xx + 3) % 4, y, 3, 1))
+
+    greeted = 28 + 2 * (z // 3 * core + (3 - z) // 3 * (1 - core))
 
     f_copy.wait()
     src = lax.broadcasted_iota(jnp.int32, (K, K), 0)
@@ -147,7 +154,7 @@
 
         @pl.when(i == 0)
         def _():
-            pl.semaphore_wait(barrier, 32)
+            pl.semaphore_wait(barrier, greeted)
 
         @pl.when(i < FLYING)
         def _():

time: 76.2 us -> 76.6 us (level)
  no operation moved by 1% of the time
where the time goes in v4:
time: 76.6 us; the launch traced here: 76.4 us
  Pallas kernels  72.7 us (95%)
  between operations  2.4 us (3%)
  local copies, waits for them, and re-layouts  1.3 us (2%)
    pallas_call x1, Pallas kernels, on_device(): pl.pallas_call(kernel, name='autocorrelation_gradient', out_shape=(jax.Sh...  72.7 us

profile of v4, /device:TPU:1, one launch (start us, length us, event | category | flops | bytes accessed | tf_op | source)
XLA Modules:
  0.0 76.4 jit_solution(11983768477561020325)
XLA Ops:
  0.6 72.7 %autocorrelation_gradient.1 = (f32[2,1024]{1,0:T(2,128)}, f32[1]{0:T(128)}) custom-call(bf16[16,512,1024]{2,1,0:T(8,128)(2,1)} %x_hbm.1, bf16[1024,128]{1,0:T(8,128)(2,1)} %f_hbm.1), custom_call_target="tpu_custom_call" | custom-call | tf_op jit(solution)/shard_map/autocorrelation_gradient/pallas_call | solution.py:609
  73.3 1.3 %copy.6 = f32[2,1024]{1,0:T(2,128)} copy(f32[2,1024]{1,0:T(2,128)} %get-tuple-element.4) | data formatting | bytes 16384
